TPU v7x, 512 devices: a whole 4x8x8 slice. The times are simulated.
512 devices in a mesh: row: 16 (over z_hi, x, core), col: 32 (over z_lo, y).
Axes of the slice: x: 4, y: 8, z: 8 (z_hi: 2, z_lo: 4; z = z_hi * 4 + z_lo), core: 2. Of those that a mesh axis runs over, the one named last changes fastest.
Arguments:
- design: bfloat16 [2048, 14080], P('row', 'col'), may hold values from -0.125 to 0.125
- nuisance_vals: float32 [4, 2048], P(None, 'row'), may hold values from -1 to 1
- arc_index: int32 [2048], P('row'), may hold values from 0 to 63, never falling along the last dimension, each value on 1 to 64 neighbouring positions
- filter_taps: float32 [128], replicated, may hold values from -0.5 to 0.5
- ordering: int32 [14336], replicated, may hold values from 0 to 14335, each once
- normal_prior: float32 [14336, 14336], P('row', 'col'), may hold values from -0.4 to 25
Outputs:
- normal_post: float32 [14336, 14336], P('row', 'col')
Inputs may be any that keep to these rules, and one draw needn't show every extreme that they name: `arc_index`: arc numbers never fall along the rows; each arc covers 1 to 64 rows. `ordering`: every slot is the image of exactly one design column.
All inputs are finite; a program needn't handle non-finite values.
Results may differ from a plain program's by a relative error of at most 0.0065.
Values may be sent and summed in bfloat16 or wider, within the bound.
A program may use at most 64 MiB of HBM per device.

v0:
```python
import jax
import jax.numpy as jnp
from jax import lax
from jax.sharding import PartitionSpec as P

NPA = 4
NUIS = 256


def shifted(block, axis, distance):
    devices = range(lax.axis_size(axis))
    route = [(i - distance, i) for i in devices if i - distance in devices]
    return lax.ppermute(block, axis, route)


def nuisance_block(nuisance_vals, arc_values):
    columns = jnp.arange(NUIS)
    selector = ((columns % NPA)[None, :] == jnp.arange(NPA)[:, None]).astype(jnp.float32)
    picked = jnp.dot(
        nuisance_vals.T,
        selector,
        precision=lax.Precision.HIGHEST,
        preferred_element_type=jnp.float32,
    )
    owners = (columns // NPA).astype(jnp.float32)
    return jnp.where(arc_values[:, None] == owners[None, :], picked, jnp.float32(0.0))


def toeplitz_taps(filter_taps, row_count):
    tap_count = filter_taps.shape[0]
    band_width = row_count + tap_count - 1
    reversed_taps = jnp.concatenate([filter_taps[::-1], jnp.zeros((row_count - 1,), jnp.float32)])
    padded_taps = jnp.concatenate([reversed_taps, jnp.zeros((row_count - 1,), jnp.float32)])
    period = padded_taps.shape[0]
    tiled = jnp.tile(padded_taps, row_count)[: row_count * (period - 1)]
    return tiled.reshape(row_count, period - 1)[:, :band_width]


def per_device(design, nuisance_vals, arc_index, filter_taps, ordering, normal_prior):
    row_count = design.shape[0]
    tap_count = filter_taps.shape[0]
    coef_width = design.shape[1]
    rim_start = row_count - tap_count + 1
    arc_values = arc_index.astype(jnp.float32)
    rim_design = shifted(design[rim_start:], "row", 1)
    rim_vals, rim_arcs = shifted((nuisance_vals[:, rim_start:], arc_values[rim_start:]), "row", 1)
    extended_vals = jnp.concatenate([rim_vals, nuisance_vals], 1)
    extended_arcs = jnp.concatenate([rim_arcs, arc_values], 0)
    extended_nuis = nuisance_block(extended_vals, extended_arcs)
    extended_design = jnp.concatenate([rim_design, design], 0)
    band = toeplitz_taps(filter_taps, row_count)
    band_high = band.astype(jnp.bfloat16)
    band_low = (band - band_high.astype(jnp.float32)).astype(jnp.bfloat16)
    design_part = jnp.dot(band_high, extended_design, preferred_element_type=jnp.float32)
    design_part = design_part + jnp.dot(
        band_low, extended_design, preferred_element_type=jnp.float32
    )
    nuis_part = jnp.dot(
        band, extended_nuis, precision=lax.Precision.HIGHEST, preferred_element_type=jnp.float32
    )
    filtered = jnp.concatenate([design_part, nuis_part], 1).astype(jnp.bfloat16)
    gathered = lax.all_gather(filtered[:, :coef_width], "col", axis=1, tiled=True)
    combined = jnp.concatenate([gathered, filtered[:, coef_width:]], 1)
    ordered = combined[:, jnp.argsort(ordering)]
    total_cols = combined.shape[1]
    row_groups = lax.axis_size("row")
    col_groups = lax.axis_size("col")
    row_share = total_cols // row_groups
    col_share = total_cols // col_groups
    panels = lax.all_to_all(
        ordered.reshape(row_count, row_groups, row_share),
        "row",
        split_axis=1,
        concat_axis=0,
        tiled=True,
    )
    panels = panels.reshape(row_count * row_groups, row_share)
    col_index = lax.axis_index("col")
    own_cols = lax.dynamic_slice_in_dim(ordered, col_index * col_share, col_share, 1)
    return normal_prior + lax.dot_general(
        panels,
        lax.all_gather(own_cols, "row", axis=0, tiled=True),
        (((0,), (0,)), ((), ())),
        preferred_element_type=jnp.float32,
    )


def solution(mesh):
    return jax.shard_map(
        per_device,
        mesh=mesh,
        in_specs=(P("row", "col"), P(None, "row"), P("row"), P(), P(), P("row", "col")),
        out_specs=P("row", "col"),
        check_vma=False,
    )
```

profile of v0, /device:TPU:75, one launch (start us, length us, event | category | flops | bytes accessed | tf_op | source)
XLA Modules:
  0.0 377.1 jit_solution(7443478387569468022)
XLA Ops:
  6.5 0.0 all-gather.3.cloned.1.call-start
  6.5 1.0 slice.23
  7.5 3.7 collective-permute-start
  11.2 0.7 rev.3
  12.0 0.2 tile.10
  12.3 0.3 reshape.35
  12.6 0.4 collective-permute-done
  13.0 1.2 fusion.3
  14.1 1.8 fusion
  16.0 0.0 all-gather.3.cloned.1.call-update
  16.0 0.7 convert_element_type.24
  16.7 0.1 slice.25
  16.7 4.3 %collective-permute-start.1 = (f32[127]{0:T(128)S(1)}, f32[127]{0:T(128)S(1)}, u32[]{:S(2)}, u32[]{:S(2)}) collective-permute-start(f32[127]{0:T(128)S(1)} %slice.25), channel_id=1, source_target_pairs={{0,32},{32,64},{64,96},{96,128},{128,160},{160,192},{192,224},{224... | collective-permute-start | bytes 1532 | tf_op jit(solution)/shard_map/ppermute | solution.py:13
  21.1 0.8 slice.26
  21.8 1.9 collective-permute-start.2
  23.7 9.0 %sort.17 = (s32[14336]{0:T(1024)}, s32[14336]{0:T(1024)S(1)}) sort(s32[14336]{0:T(1024)} %param.10, s32[14336]{0:T(1024)S(1)} %iota.18), dimensions={0}, to_apply=%region_0.1 | sort | flops 200704 | bytes 229376 | tf_op jit(solution)/shard_map/jit(argsort)/sort | solution.py:64
  32.8 0.0 collective-permute-done.1
  32.8 0.1 pad_maximum_fusion.4
  32.8 0.0 collective-permute-done.2
  32.8 1.1 fusion.9
  33.9 0.7 convolution_convert_fusion
  34.6 116.8 %all-gather.3.cloned.1.call-done = bf16[128,14080]{0,1:T(8,128)(2,1)} async-done(((bf16[128,440]{0,1:T(8,128)(2,1)}), bf16[128,14080]{0,1:T(8,128)(2,1)}) %all-gather.3.cloned.1.call-update) | async-done | bytes 3604496 | tf_op jit(solution)/shard_map/all_gather | solution.py:62
  151.4 9.4 %pad_maximum_fusion = bf16[128,14336]{0,1:T(8,128)(2,1)} fusion(bf16[128,256]{0,1:T(8,128)(2,1)S(1)} %convolution_convert_fusion, bf16[128,14080]{0,1:T(8,128)(2,1)} %all-gather.3.cloned.1.call-done), kind=kLoop, calls=%fused_computation.1 | loop fusion | flops 7340032 | bytes 7340032 | tf_op jit(solution)/shard_map/concatenate | solution.py:63
  160.8 51.3 %gather_fusion = bf16[14336,128]{1,0:T(8,128)(2,1)} fusion(bf16[128,14336]{0,1:T(8,128)(2,1)} %pad_maximum_fusion, s32[14336]{0:T(1024)S(1)} %fusion.8), kind=kCustom, calls=%fused_computation | custom fusion | bytes 7397376 | tf_op jit(solution)/shard_map/gather | solution.py:64
  212.1 6.1 %copy.9 = bf16[128,16,896]{2,0,1:T(8,128)(2,1)} copy(bf16[128,16,896]{0,2,1:T(8,128)(2,1)} %bitcast.13) | data formatting | bytes 7340032 | tf_op jit(solution)/shard_map/reshape | solution.py:71
  218.2 0.0 copy-start
  218.2 29.0 %all-to-all-start = ((bf16[128,16,896]{2,0,1:T(8,128)(2,1)}), bf16[128,16,896]{2,0,1:T(8,128)(2,1)}, u32[]{:S(2)}, u32[]{:S(2)}) async-start(bf16[128,16,896]{2,0,1:T(8,128)(2,1)} %copy.9), calls=%async_computation | async-start | bytes 7340032 | tf_op jit(solution)/shard_map/all_to_all | solution.py:70
  247.2 0.0 all-gather.5.cloned.1.call-start
  247.2 1.6 dynamic-slice_bitcast_fusion
  248.8 0.0 all-gather.5.cloned.1.call-update
  248.8 115.6 %all-gather.5.cloned.1.call-done = bf16[2048,448]{0,1:T(8,128)(2,1)} async-done(((bf16[128,448]{0,1:T(8,128)(2,1)}), bf16[2048,448]{0,1:T(8,128)(2,1)}) %all-gather.5.cloned.1.call-update) | async-done | bytes 1835024 | tf_op jit(solution)/shard_map/all_gather | solution.py:82
  364.4 0.0 all-to-all-done
  364.4 0.0 copy-done
  364.4 5.8 %convolution_add_fusion = f32[896,448]{0,1:T(8,128)} fusion(f32[896,448]{0,1:T(8,128)S(1)} %copy-done, bf16[2048,448]{0,1:T(8,128)(2,1)} %all-gather.5.cloned.1.call-done, bf16[2048,896]{1,0:T(8,128)(2,1)} %bitcast.4), kind=kOutput, calls=%fused_computation.2 | convolution fusion | flops 1644568576 | bytes 8716288 | tf_op jit(solution)/shard_map/dot_general | solution.py:80
  (6 shorter events, 0.1 us)
Async XLA Ops:
  6.5 144.9 %all-gather.3.cloned.1.call-start = ((), (), s32[]{:S(2)}) async-start(), calls=%async_computation.1 | async-start | bytes 3717120 | tf_op jit(solution)/shard_map/all_gather | solution.py:62
  7.5 5.4 %collective-permute-start = (bf16[127,440]{0,1:T(8,128)(2,1)S(1)}, bf16[127,440]{0,1:T(8,128)(2,1)S(1)}, u32[]{:S(2)}, u32[]{:S(2)}) collective-permute-start(bf16[127,440]{0,1:T(8,128)(2,1)S(1)} %slice.23), channel_id=1, source_target_pairs={{0,32},{32,64},{64,96},{96,128},{128,160},{160,192},{192,224},{224... | collective-permute-start | bytes 335288 | tf_op jit(solution)/shard_map/ppermute | solution.py:13
  16.7 16.0 %collective-permute-start.1 = (f32[127]{0:T(128)S(1)}, f32[127]{0:T(128)S(1)}, u32[]{:S(2)}, u32[]{:S(2)}) collective-permute-start(f32[127]{0:T(128)S(1)} %slice.25), channel_id=1, source_target_pairs={{0,32},{32,64},{64,96},{96,128},{128,160},{160,192},{192,224},{224... | collective-permute-start | bytes 1532 | tf_op jit(solution)/shard_map/ppermute | solution.py:13
  21.8 11.0 %collective-permute-start.2 = (f32[4,127]{1,0:T(4,128)S(1)}, f32[4,127]{1,0:T(4,128)S(1)}, u32[]{:S(2)}, u32[]{:S(2)}) collective-permute-start(f32[4,127]{1,0:T(4,128)S(1)} %slice.26), channel_id=1, source_target_pairs={{0,32},{32,64},{64,96},{96,128},{128,160},{160,192},{192,224},{224... | collective-permute-start | bytes 6104 | tf_op jit(solution)/shard_map/ppermute | solution.py:13
  218.2 146.3 %copy-start = (f32[896,448]{0,1:T(8,128)S(1)}, f32[896,448]{0,1:T(8,128)}, u32[]{:S(2)}) copy-start(f32[896,448]{0,1:T(8,128)} %param.11) | copy-start | bytes 4816900
  218.2 146.3 %all-to-all-start = ((bf16[128,16,896]{2,0,1:T(8,128)(2,1)}), bf16[128,16,896]{2,0,1:T(8,128)(2,1)}, u32[]{:S(2)}, u32[]{:S(2)}) async-start(bf16[128,16,896]{2,0,1:T(8,128)(2,1)} %copy.9), calls=%async_computation | async-start | bytes 7340032 | tf_op jit(solution)/shard_map/all_to_all | solution.py:70
  247.2 117.3 %all-gather.5.cloned.1.call-start = ((), (), s32[]{:S(2)}) async-start(), calls=%async_computation.2 | async-start | bytes 1949696 | tf_op jit(solution)/shard_map/all_gather | solution.py:82
Sparse Core Ops, SparseCore 0:
  16.1 135.2 all-gather.2
  251.1 113.2 all-gather.4
where the time goes:
time: 378 us; the launch traced here: 377 us
  waiting for transfers between devices  233 us (62%)
  local copies, waits for them, and re-layouts  62.1 us (16%)
  starting transfers between devices  38.9 us (10%)
  other arithmetic  19.1 us (5%)
  between operations  13.5 us (4%)
  matrix products  10.5 us (3%)
    all_gather x1, waiting for transfers between devices, per_device(): lax.all_gather(filtered[:, :coef_width], 'col', axis=1, tiled=True)  117 us
    all_gather x1, waiting for transfers between devices, per_device(): lax.all_gather(own_cols, 'row', axis=0, tiled=True)  116 us
    gather x1, local copies, waits for them, and re-layouts, per_device(): ordered = combined[:, jnp.argsort(ordering)]  51.3 us
    all_to_all x1, starting transfers between devices, per_device(): lax.all_to_all(ordered.reshape(row_count, row_groups, row_share), 'row',...  29 us
    ppermute x3, starting transfers between devices, shifted(): return lax.ppermute(block, axis, route)  9.91 us
    concatenate x1, other arithmetic, per_device(): combined = jnp.concatenate([gathered, filtered[:, coef_width:]], 1)  9.37 us
    sort x1, other arithmetic, per_device(): ordered = combined[:, jnp.argsort(ordering)]  8.98 us
  transfers between devices with their start and end apart: 6, of which 3 were waited for; matrix products, arithmetic and copies ran while one was open for 4% of the time, Pallas kernels for 0%

commit v1 on v0

v1 whole, which is shorter than its diff:
```python
import jax
import jax.numpy as jnp
from jax import lax
from jax.experimental import pallas as pl
from jax.experimental.pallas import tpu as pltpu
from jax.sharding import PartitionSpec as P

MESH = pl.DeviceIdType.MESH
F32, BF16 = jnp.float32, jnp.bfloat16

ROWS, COLS = 16, 32
NPA, NUIS = 4, 256
SEG = 128
COEF_W = 440
TT = 4
RSH, CSH = 896, 448
GROUPS, GTILES = 16, 8


def nt(a, b):
    return lax.dot_general(a, b, (((1,), (1,)), ((), ())), preferred_element_type=F32)


def nn(a, b):
    return lax.dot_general(a, b, (((1,), (0,)), ((), ())), preferred_element_type=F32)


def iota(shape, dim):
    return lax.broadcasted_iota(jnp.int32, shape, dim)


def remote(src, dst, send_sem, recv_sem, row, col):
    return pltpu.make_async_remote_copy(
        src_ref=src,
        dst_ref=dst,
        send_sem=send_sem,
        recv_sem=recv_sem,
        device_id=(row, col),
        device_id_type=MESH,
    )


def kernel(
    design,
    vals,
    arcs,
    taps,
    slots,
    prior,
    out,
    own,
    halo,
    nown,
    nhalo,
    wbuf,
    p1,
    hot_hi,
    hot_lo,
    xg,
    oacc,
    obuf,
    a2,
    b2,
    btw,
    abuf,
    bbuf,
    hsend,
    hrecv,
    psend,
    precv,
    asend,
    arecv,
    bsend,
    brecv,
    gsend,
    grecv,
    qsend,
    qrecv,
    prior_sem,
):
    r, c = lax.axis_index("row"), lax.axis_index("col")
    y, zl0 = c % 8, c // 8
    xi = (r // 2) % 4
    rbase = r - 2 * xi
    r_core = r + 1 - 2 * (r % 2)
    r_z = (r + 8) % ROWS
    r_next, r_prev = (r + 1) % ROWS, (r + ROWS - 1) % ROWS

    def r_x(row, d):
        return row - 2 * xi + 2 * ((xi + d) % 4)

    half, slot_in_half = c // 16, c % 16
    a_col = 2 * r + half
    src_row, src_col = c // 2, 16 * (c % 2)
    is_self = (src_row == r) & (half == c % 2)

    prior_copy = pltpu.make_async_copy(prior, out, prior_sem)
    prior_copy.start()

    barrier = pltpu.get_barrier_semaphore()

    def tell(row, col):
        pl.semaphore_signal(barrier, inc=1, device_id=(row, col), device_id_type=MESH)

    tell(r_prev, c)
    for d in (1, 2, 3):
        tell(r_x(r, d), c)
    tell(r_core, c)
    tell(r_z, c)

    @pl.loop(1, COLS)
    def _(i):
        tell(r, (c + i) % COLS)

    @pl.loop(0, 16)
    def _(i):
        @pl.when(jnp.logical_not(is_self & (i == slot_in_half)))
        def _():
            tell(src_row, src_col + i)

    own[...] = jnp.zeros((512, SEG), BF16)
    own[0:COEF_W, :] = design[...]
    nown[0:4, :] = vals[...]
    nown[4:8, :] = jnp.broadcast_to(arcs[...].astype(F32), (4, SEG))

    pl.semaphore_wait(barrier, 52 + 1 - is_self.astype(jnp.int32))

    halo_copies = [
        remote(own.at[pl.ds(0, 448)], halo.at[pl.ds(0, 448)], hsend.at[0], hrecv.at[0], r_next, c),
        remote(nown, nhalo, hsend.at[1], hrecv.at[1], r_next, c),
    ]
    for copy in halo_copies:
        copy.start()

    hp = (iota((256, 128), 0) // 4).astype(F32)
    lp = iota((256, 128), 0).astype(F32)

    def factors(rows):
        s = rows.astype(F32)
        seg = jnp.floor((s + 0.5) * (1.0 / RSH))
        w = s - seg * RSH
        h = jnp.floor((w + 0.5) * (1.0 / 256.0))
        return jnp.where(rows < 0, -1.0, 4.0 * seg + h), w - 256.0 * h

    def one_hot(row, pattern):
        return jnp.where(jnp.broadcast_to(row, pattern.shape) == pattern, 1.0, 0.0).astype(BF16)

    @pl.loop(0, GROUPS)
    def _(g):
        hi, lo = factors(slots[pl.ds(pl.multiple_of(8 * g, 8), 8), :])
        for i in range(GTILES):
            hot_hi[g, :, 128 * i : 128 * i + 128] = one_hot(hi[i : i + 1], hp)
            hot_lo[g, :, 128 * i : 128 * i + 128] = one_hot(lo[i : i + 1], lp)

    line = jnp.concatenate([taps[...], jnp.zeros((1, SEG), F32)], 1)
    band = pltpu.roll(jnp.broadcast_to(line, (SEG, 2 * SEG)), 0, 1, stride=1, stride_axis=0)
    has_past = jnp.where(r > 0, 1.0, 0.0).astype(F32)
    band_now, band_past = band[:, :SEG], band[:, SEG:] * has_past

    def split(x):
        high = x.astype(BF16)
        return high, (x - high.astype(F32)).astype(BF16)

    now_hi, now_lo = split(band_now)
    past_hi, past_lo = split(band_past)

    for copy in halo_copies:
        copy.wait()

    mine = own[...]
    past = halo[0:448, :]
    filtered = nn(mine, now_hi) + nn(mine, now_lo)
    part = nn(past, past_hi) + nn(past, past_lo)
    filtered = jnp.concatenate([filtered[0:448] + part, filtered[448:512]], 0).astype(BF16)
    p_row, p_time = iota((512, 128), 0), iota((512, 128), 1)
    at_time = p_time == TT * (p_row // 16) + p_row % 4
    wsum = jnp.zeros((512, 128), F32)
    for q in range(4):
        pick = jnp.where(at_time & ((p_row // 4) % 4 == q), 1.0, 0.0).astype(BF16)
        wsum = wsum + nt(pick, filtered[128 * q : 128 * q + 128])
    wbuf[...] = wsum.astype(BF16).reshape(COLS, 16, 128)

    p1[c] = wbuf[c]

    @pl.loop(1, COLS)
    def _(i):
        to = (c + i) % COLS
        remote(wbuf.at[to], p1.at[c], psend.at[i], precv.at[c], r, to).start()

    n_row = iota((NUIS, SEG), 0)

    def nuisance(ref):
        v = jnp.broadcast_to(ref[0:1], (NUIS, SEG))
        for q in range(1, NPA):
            v = jnp.where(n_row % NPA == q, jnp.broadcast_to(ref[q : q + 1], (NUIS, SEG)), v)
        arc = jnp.broadcast_to(ref[4:5], (NUIS, SEG))
        return jnp.where(arc == (n_row // NPA).astype(F32), v, 0.0)

    def exact(a, b):
        return lax.dot_general(
            a, b, (((1,), (0,)), ((), ())), precision=lax.Precision.HIGHEST, preferred_element_type=F32
        )

    nfil = (exact(nuisance(nown), band_now) + exact(nuisance(nhalo), band_past)).astype(BF16)
    s_row, s_time = iota((16, 128), 0), iota((16, 128), 1)
    pick = jnp.where(s_time == TT * c + s_row % 4, 1.0, 0.0).astype(BF16)
    nhi, nlo = factors(slots[128:136, :])
    accum = jnp.zeros((256, 256), F32)
    for q in range(2):
        rep = nt(pick, nfil[128 * q : 128 * q + 128]).astype(BF16)
        x = jnp.concatenate([rep] * 16, 0) * one_hot(nhi[q : q + 1], hp)
        accum = accum + nt(x, one_hot(nlo[q : q + 1], lp))
    oacc[...] = accum

    @pl.loop(1, COLS)
    def _(i):
        src = (c + COLS - i) % COLS
        remote(wbuf.at[src], p1.at[src], psend.at[i], precv.at[src], r, src).wait()

    low4 = iota((8, 128), 0) < 4

    @pl.loop(0, GROUPS)
    def _(g):
        for k in range(2):
            msg = p1[2 * g + k].astype(F32)
            for v in range(2):
                part = msg[8 * v : 8 * v + 8]
                rot = pltpu.roll(part, 4, 0)
                for u in range(2):
                    rep = jnp.where(low4, part, rot) if u == 0 else jnp.where(low4, rot, part)
                    rep = jnp.concatenate([rep, rep], 0).astype(BF16)
                    i = 4 * k + 2 * v + u
                    lanes = slice(128 * i, 128 * i + 128)
                    xg[:, lanes] = jnp.concatenate([rep] * 16, 0) * hot_hi[g, :, lanes]
        oacc[...] += nt(xg[...], hot_lo[g])

    obuf[...] = oacc[...].astype(BF16).reshape(16, 16, 256)

    @pl.loop(0, 16)
    def _(i):
        to = (r + i) % ROWS
        here = is_self & (i == 0)

        @pl.when(here)
        def _():
            a2[slot_in_half] = obuf[r]

        @pl.when(jnp.logical_not(here))
        def _():
            remote(obuf.at[to], a2.at[slot_in_half], asend.at[i], arecv.at[slot_in_half], to, a_col).start()

    b2[c] = obuf[c // 2]

    @pl.loop(1, COLS)
    def _(i):
        to = (c + i) % COLS
        remote(obuf.at[to // 2], b2.at[c], bsend.at[i], brecv.at[c], r, to).start()

    @pl.loop(0, 16)
    def _(i):
        here = is_self & (i == slot_in_half)

        @pl.when(jnp.logical_not(here))
        def _():
            remote(obuf.at[i], a2.at[i], asend.at[i], arecv.at[i], src_row, src_col + i).wait_recv()

    @pl.loop(0, 16)
    def _(i):
        to = (r + i) % ROWS

        @pl.when(jnp.logical_not(is_self & (i == 0)))
        def _():
            remote(obuf.at[to], a2.at[i], asend.at[i], arecv.at[i], to, a_col).wait_send()

    def chunk(zl, yy):
        return abuf.at[zl * 4 + yy // 2, pl.ds(pl.multiple_of(64 * (yy % 2), 64), 64)]

    a_in = a2[...].reshape(256, 256)
    m, p = iota((64, 256), 0), iota((64, 256), 1)
    for h in range(4):
        pick = jnp.where(p == 16 * (m // 4) + 4 * h + m % 4, 1.0, 0.0).astype(BF16)
        width = 256 if h < 3 else 128
        piece = nn(pick, a_in[:, :width]).astype(BF16)
        abuf[c // 2, pl.ds(pl.multiple_of(64 * (c % 2), 64), 64), 256 * h : 256 * h + width] = piece

    y_of = [(y + d) % 8 for d in range(8)]
    zls = [(zl0 + k) % 4 for k in range(4)]
    sends = []

    def pass_on(k, dist, direction):
        yy = y_of[(-direction * dist) % 8]
        n = len(sends)
        copy = remote(
            chunk(zls[k], yy),
            chunk(zls[k], yy),
            gsend.at[n],
            grecv.at[zls[k] * 8 + yy],
            r,
            zl0 * 8 + y_of[direction % 8],
        )
        copy.start()
        sends.append(copy)

    def arrived(zl, yy):
        remote(chunk(zl, yy), chunk(zl, yy), gsend.at[0], grecv.at[zl * 8 + yy], r, c).wait_recv()

    pass_on(0, 0, 1)
    pass_on(0, 0, -1)
    for k in (1, 3, 2):
        copy = remote(
            chunk(zl0, y), chunk(zl0, y), gsend.at[len(sends)], grecv.at[c], r, zls[k] * 8 + y
        )
        copy.start()
        sends.append(copy)

    @pl.loop(1, COLS)
    def _(i):
        src = (c + COLS - i) % COLS
        remote(obuf.at[0], b2.at[src], bsend.at[i], brecv.at[src], r, src).wait()

    b_in = b2[...].reshape(512, 256)
    m, p = iota((128, 512), 0), iota((128, 512), 1)
    for h in range(4):
        pick = jnp.where(p == 16 * (m // 4) + 4 * h + m % 4, 1.0, 0.0).astype(BF16)
        width = 256 if h < 3 else 128
        btw[256 * h : 256 * h + width, :] = nn(pick, b_in[:, :width]).T.astype(BF16)
    bbuf[r] = btw[pl.ds(pl.multiple_of(CSH * (c % 2), 64), CSH), :]

    bsends = []

    def spread(row, to):
        n = len(bsends)
        copy = remote(bbuf.at[row], bbuf.at[row], qsend.at[n], qrecv.at[row], to, c)
        copy.start()
        bsends.append(copy)

    def b_arrived(row):
        remote(bbuf.at[row], bbuf.at[row], qsend.at[0], qrecv.at[row], r, c).wait_recv()

    spread(r, r_z)
    for d in (1, 3, 2):
        spread(r, r_x(r, d))
    spread(r, r_core)

    for k in (1, 3, 2):
        arrived(zls[k], y)
        pass_on(k, 0, 1)
        pass_on(k, 0, -1)

    b_arrived(r_z)
    for d in (1, 3, 2):
        spread(r_z, r_x(r, d))
    spread(r_z, r_core)

    def product(k, pair):
        idx = zls[k] * 4 + pair
        out[...] += nn(bbuf[idx], abuf[idx])

    pair0 = y // 2
    for s in range(1, 5):
        for k in range(4):
            right, left = (4, 3) if k % 2 == 0 else (3, 4)
            if s <= right:
                arrived(zls[k], y_of[-s % 8])
                if s < right:
                    pass_on(k, s, 1)
            if s <= left:
                arrived(zls[k], y_of[s % 8])
                if s < left:
                    pass_on(k, s, -1)
            if s == 2:
                product(k, pair0)
            if s == 3:
                product(k, (pair0 + 1) % 4)
                product(k, (pair0 + 3) % 4)
            if s == 4:
                product(k, (pair0 + 2) % 4)
        if s == 1:
            for base in (r, r_z):
                for d in (1, 3, 2):
                    b_arrived(r_x(base, d))
                    spread(r_x(base, d), r_core)
            for base in (r, r_z):
                for d in range(4):
                    row = r_x(base, d)
                    b_arrived(row + 1 - 2 * (row % 2))
            prior_copy.wait()

    for copy in sends + bsends:
        copy.wait_send()


def per_device(design, nuisance_vals, arc_index, filter_taps, ordering, normal_prior):
    coef = COEF_W * COLS
    cols = jnp.pad(ordering[:coef].reshape(COLS, COEF_W), ((0, 0), (0, 512 - COEF_W)), constant_values=-1)
    slots = jnp.concatenate(
        [cols.reshape(128, 128), ordering[coef:].reshape(2, 128), jnp.full((6, 128), -1, jnp.int32)], 0
    )
    vmem = pl.BlockSpec(memory_space=pltpu.VMEM)
    dma = pltpu.SemaphoreType.DMA
    result = pl.pallas_call(
        kernel,
        out_shape=jax.ShapeDtypeStruct((CSH, RSH), F32),
        in_specs=[vmem] * 5 + [pl.BlockSpec(memory_space=pl.ANY)],
        out_specs=vmem,
        scratch_shapes=[
            pltpu.VMEM((512, SEG), BF16),
            pltpu.VMEM((512, SEG), BF16),
            pltpu.VMEM((8, SEG), F32),
            pltpu.VMEM((8, SEG), F32),
            pltpu.VMEM((COLS, 16, 128), BF16),
            pltpu.VMEM((COLS, 16, 128), BF16),
            pltpu.VMEM((GROUPS, 256, 128 * GTILES), BF16),
            pltpu.VMEM((GROUPS, 256, 128 * GTILES), BF16),
            pltpu.VMEM((256, 128 * GTILES), BF16),
            pltpu.VMEM((256, 256), F32),
            pltpu.VMEM((16, 16, 256), BF16),
            pltpu.VMEM((16, 16, 256), BF16),
            pltpu.VMEM((32, 16, 256), BF16),
            pltpu.VMEM((RSH, SEG), BF16),
            pltpu.VMEM((16, SEG, RSH), BF16),
            pltpu.VMEM((16, CSH, SEG), BF16),
            dma((2,)),
            dma((2,)),
            dma((COLS,)),
            dma((COLS,)),
            dma((16,)),
            dma((16,)),
            dma((COLS,)),
            dma((COLS,)),
            dma((40,)),
            dma((COLS,)),
            dma((20,)),
            dma((ROWS,)),
            dma,
        ],
        compiler_params=pltpu.CompilerParams(
            collective_id=0, has_side_effects=True, vmem_limit_bytes=48 * 1024 * 1024
        ),
    )(
        design.T,
        nuisance_vals,
        arc_index.reshape(1, SEG),
        filter_taps.reshape(1, SEG),
        slots,
        normal_prior.T,
    )
    return result.T


def solution(mesh):
    return jax.shard_map(
        per_device,
        mesh=mesh,
        in_specs=(P("row", "col"), P(None, "row"), P("row"), P(), P(), P("row", "col")),
        out_specs=P("row", "col"),
        check_vma=False,
    )
```

time: 378 us -> 112 us (0.30)
  the two profiles are of different devices: /device:TPU:75 before, /device:TPU:6 now
where the time goes in v1:
time: 112 us; the launch traced here: 111 us
  Pallas kernels  103 us (92%)
  local copies, waits for them, and re-layouts  7.15 us (6%)
    pallas_call x1, Pallas kernels, per_device(): pl.pallas_call(kernel, out_shape=jax.ShapeDtypeStruct((CSH, RSH), F32), i...  103 us
    unnamed x11, local copies, waits for them, and re-layouts  5.46 us

profile of v1, /device:TPU:6, one launch (start us, length us, event | category | flops | bytes accessed | tf_op | source)
XLA Modules:
  0.0 110.8 jit_solution(16120526878682712932)
XLA Ops:
  0.0 0.1 pad.7.clone
  0.1 0.7 slice_bitcast_fusion
  0.8 0.9 reshape.23
  1.7 0.1 add_add_fusion.slots
  1.8 0.0 copy-start
  1.8 1.4 %copy-done = f32[896,448]{0,1:T(8,128)S(1)} copy-done((f32[896,448]{0,1:T(8,128)S(1)}, f32[896,448]{0,1:T(8,128)}, u32[]{:S(2)}) %copy-start) | copy-done | bytes 1605656
  3.2 0.0 copy-start.1
  3.2 0.9 copy-done.1
  4.1 0.0 copy-start.2
  4.1 0.7 copy-done.2
  4.8 0.0 copy-start.3
  4.8 0.7 copy-done.3
  5.5 0.0 copy-start.4
  5.5 0.7 copy-done.4
  6.1 103.5 %shard_map.64 = f32[448,896]{1,0:T(8,128)S(1)} custom-call(bf16[440,128]{1,0:T(8,128)(2,1)S(1)} %bitcast.10, f32[4,128]{1,0:T(4,128)S(1)} %copy-done.2, s32[1,128]{1,0:T(1,128)S(1)} %bitcast.11, f32[1,128]{1,0:T(1,128)S(1)} %bitcast.12, s32[136,128]{1,0:T(8,128)S(1)} %add_add_fusion.slots, f32[448,896]{1,0:T(8,128)S(1)} %bitcast.9), custom_call_target="tpu_custom_call" | custom-call | tf_op jit(solution)/shard_map/pallas_call | solution.py:401
  109.6 1.2 %copy.8 = f32[896,448]{0,1:T(8,128)} copy(f32[896,448]{0,1:T(8,128)S(1)} %bitcast.8) | data formatting | bytes 3211264
  (3 shorter events, 0.0 us)
Async XLA Ops:
  1.8 1.4 %copy-start = (f32[896,448]{0,1:T(8,128)S(1)}, f32[896,448]{0,1:T(8,128)}, u32[]{:S(2)}) copy-start(f32[896,448]{0,1:T(8,128)} %param.11) | copy-start | bytes 4816900
  3.2 0.9 copy-start.1
  4.1 0.7 copy-start.2
  4.8 0.7 copy-start.3
  5.5 0.7 copy-start.4

commit v2 on v1

--- a/solution.py
+++ b/solution.py
@@ -42,12 +42,16 @@
 
 def kernel(
     design,
+    vals_hbm,
+    arcs_hbm,
+    taps_hbm,
+    ordering_hbm,
+    out,
     vals,
     arcs,
     taps,
+    ordering,
     slots,
-    prior,
-    out,
     own,
     halo,
     nown,
@@ -61,9 +65,10 @@
     obuf,
     a2,
     b2,
-    btw,
     abuf,
     bbuf,
+    btr,
+    load_sem,
     hsend,
     hrecv,
     psend,
@@ -76,7 +81,6 @@
     grecv,
     qsend,
     qrecv,
-    prior_sem,
 ):
     r, c = lax.axis_index("row"), lax.axis_index("col")
     y, zl0 = c % 8, c // 8
@@ -89,41 +93,37 @@
     def r_x(row, d):
         return row - 2 * xi + 2 * ((xi + d) % 4)
 
-    half, slot_in_half = c // 16, c % 16
-    a_col = 2 * r + half
-    src_row, src_col = c // 2, 16 * (c % 2)
-    is_self = (src_row == r) & (half == c % 2)
-
-    prior_copy = pltpu.make_async_copy(prior, out, prior_sem)
-    prior_copy.start()
+    loads = [
+        pltpu.make_async_copy(src, dst, load_sem.at[n])
+        for n, (src, dst) in enumerate(
+            ((vals_hbm, vals), (arcs_hbm, arcs), (taps_hbm, taps), (ordering_hbm, ordering))
+        )
+    ]
+    for load in loads:
+        load.start()
 
     barrier = pltpu.get_barrier_semaphore()
 
     def tell(row, col):
         pl.semaphore_signal(barrier, inc=1, device_id=(row, col), device_id_type=MESH)
 
-    tell(r_prev, c)
-    for d in (1, 2, 3):
-        tell(r_x(r, d), c)
-    tell(r_core, c)
-    tell(r_z, c)
+    @pl.loop(1, ROWS)
+    def _(i):
+        tell((r + i) % ROWS, c)
 
     @pl.loop(1, COLS)
     def _(i):
         tell(r, (c + i) % COLS)
 
-    @pl.loop(0, 16)
-    def _(i):
-        @pl.when(jnp.logical_not(is_self & (i == slot_in_half)))
-        def _():
-            tell(src_row, src_col + i)
-
+    out[...] = jnp.zeros((CSH, RSH), F32)
     own[...] = jnp.zeros((512, SEG), BF16)
     own[0:COEF_W, :] = design[...]
+    for load in loads:
+        load.wait()
     nown[0:4, :] = vals[...]
     nown[4:8, :] = jnp.broadcast_to(arcs[...].astype(F32), (4, SEG))
 
-    pl.semaphore_wait(barrier, 52 + 1 - is_self.astype(jnp.int32))
+    pl.semaphore_wait(barrier, ROWS + COLS - 2)
 
     halo_copies = [
         remote(own.at[pl.ds(0, 448)], halo.at[pl.ds(0, 448)], hsend.at[0], hrecv.at[0], r_next, c),
@@ -132,15 +132,30 @@
     for copy in halo_copies:
         copy.start()
 
+    lane = iota((1, 128), 1)
+    for src in range(COLS):
+        for q in range(4):
+            first = COEF_W * src + 128 * q
+            tile, off = first // 128, first % 128
+            line = ordering[tile : tile + 1]
+            if off:
+                line = jnp.where(lane >= off, line, ordering[tile + 1 : tile + 2])
+                line = pltpu.roll(line, 128 - off, 1)
+            if q == 3:
+                line = jnp.where(lane < COEF_W - 384, line, -1)
+            slots[4 * src + q : 4 * src + q + 1] = line
+    slots[128:130] = ordering[COLS * COEF_W // 128 :]
+
     hp = (iota((256, 128), 0) // 4).astype(F32)
     lp = iota((256, 128), 0).astype(F32)
 
     def factors(rows):
         s = rows.astype(F32)
-        seg = jnp.floor((s + 0.5) * (1.0 / RSH))
-        w = s - seg * RSH
-        h = jnp.floor((w + 0.5) * (1.0 / 256.0))
-        return jnp.where(rows < 0, -1.0, 4.0 * seg + h), w - 256.0 * h
+        cc = jnp.floor((s + 0.5) * (1.0 / CSH))
+        odd = cc - 2.0 * jnp.floor(cc * 0.5)
+        u = s - cc * CSH + 64.0 * odd
+        h = jnp.floor((u + 0.5) * (1.0 / 256.0))
+        return jnp.where(rows < 0, -1.0, 2.0 * cc + h), u - 256.0 * h
 
     def one_hot(row, pattern):
         return jnp.where(jnp.broadcast_to(row, pattern.shape) == pattern, 1.0, 0.0).astype(BF16)
@@ -204,7 +219,7 @@
     nfil = (exact(nuisance(nown), band_now) + exact(nuisance(nhalo), band_past)).astype(BF16)
     s_row, s_time = iota((16, 128), 0), iota((16, 128), 1)
     pick = jnp.where(s_time == TT * c + s_row % 4, 1.0, 0.0).astype(BF16)
-    nhi, nlo = factors(slots[128:136, :])
+    nhi, nlo = factors(slots[128:130, :])
     accum = jnp.zeros((256, 256), F32)
     for q in range(2):
         rep = nt(pick, nfil[128 * q : 128 * q + 128]).astype(BF16)
@@ -234,54 +249,39 @@
                     xg[:, lanes] = jnp.concatenate([rep] * 16, 0) * hot_hi[g, :, lanes]
         oacc[...] += nt(xg[...], hot_lo[g])
 
-    obuf[...] = oacc[...].astype(BF16).reshape(16, 16, 256)
-
-    @pl.loop(0, 16)
+    for cc in range(COLS):
+        block = oacc[8 * cc : 8 * cc + 8]
+        obuf[cc] = jnp.concatenate([block[:, :128], block[:, 128:]], 0).astype(BF16)
+
+    @pl.loop(1, ROWS)
     def _(i):
         to = (r + i) % ROWS
-        here = is_self & (i == 0)
-
-        @pl.when(here)
-        def _():
-            a2[slot_in_half] = obuf[r]
-
-        @pl.when(jnp.logical_not(here))
-        def _():
-            remote(obuf.at[to], a2.at[slot_in_half], asend.at[i], arecv.at[slot_in_half], to, a_col).start()
-
-    b2[c] = obuf[c // 2]
+        remote(obuf.at[pl.ds(2 * to, 2)], a2.at[r], asend.at[i], arecv.at[r], to, c).start()
 
     @pl.loop(1, COLS)
     def _(i):
         to = (c + i) % COLS
-        remote(obuf.at[to // 2], b2.at[c], bsend.at[i], brecv.at[c], r, to).start()
-
-    @pl.loop(0, 16)
-    def _(i):
-        here = is_self & (i == slot_in_half)
-
-        @pl.when(jnp.logical_not(here))
-        def _():
-            remote(obuf.at[i], a2.at[i], asend.at[i], arecv.at[i], src_row, src_col + i).wait_recv()
-
-    @pl.loop(0, 16)
-    def _(i):
-        to = (r + i) % ROWS
-
-        @pl.when(jnp.logical_not(is_self & (i == 0)))
-        def _():
-            remote(obuf.at[to], a2.at[i], asend.at[i], arecv.at[i], to, a_col).wait_send()
+        remote(obuf.at[to], b2.at[c], bsend.at[i], brecv.at[c], r, to).start()
+
+    a2[r] = obuf[pl.ds(2 * r, 2)]
+    b2[c] = obuf[c]
+
+    m, p = iota((448, 512), 0), iota((448, 512), 1)
+    tile = 3 * ((p // 16) % 2) + 2 * ((p // 4) % 2) + (p // 8) % 2
+    same = (p // 32 == (m % 64) // 4) & (p % 4 == m % 4)
+    pick = jnp.where(same & (tile == m // 64), 1.0, 0.0).astype(BF16)
+
+    @pl.loop(1, ROWS)
+    def _(i):
+        src = (r + ROWS - i) % ROWS
+        remote(a2.at[src], a2.at[src], asend.at[i], arecv.at[src], src, c).wait()
+
+    pieces = nn(pick, a2[...].reshape(512, 128)).astype(BF16)
+    for j in range(7):
+        abuf[c, :, 128 * j : 128 * j + 128] = pieces[64 * j : 64 * j + 64]
 
     def chunk(zl, yy):
-        return abuf.at[zl * 4 + yy // 2, pl.ds(pl.multiple_of(64 * (yy % 2), 64), 64)]
-
-    a_in = a2[...].reshape(256, 256)
-    m, p = iota((64, 256), 0), iota((64, 256), 1)
-    for h in range(4):
-        pick = jnp.where(p == 16 * (m // 4) + 4 * h + m % 4, 1.0, 0.0).astype(BF16)
-        width = 256 if h < 3 else 128
-        piece = nn(pick, a_in[:, :width]).astype(BF16)
-        abuf[c // 2, pl.ds(pl.multiple_of(64 * (c % 2), 64), 64), 256 * h : 256 * h + width] = piece
+        return abuf.at[zl * 8 + yy]
 
     y_of = [(y + d) % 8 for d in range(8)]
     zls = [(zl0 + k) % 4 for k in range(4)]
@@ -313,18 +313,19 @@
         copy.start()
         sends.append(copy)
 
+    m, p = iota((512, 512), 0), iota((512, 512), 1)
+    tile = 2 * ((p // 4) % 2) + (p // 8) % 2
+    same = (p // 16 == (m % 128) // 4) & (p % 4 == m % 4)
+    pick = jnp.where(same & (tile == m // 128), 1.0, 0.0).astype(BF16)
+
     @pl.loop(1, COLS)
     def _(i):
         src = (c + COLS - i) % COLS
-        remote(obuf.at[0], b2.at[src], bsend.at[i], brecv.at[src], r, src).wait()
-
-    b_in = b2[...].reshape(512, 256)
-    m, p = iota((128, 512), 0), iota((128, 512), 1)
-    for h in range(4):
-        pick = jnp.where(p == 16 * (m // 4) + 4 * h + m % 4, 1.0, 0.0).astype(BF16)
-        width = 256 if h < 3 else 128
-        btw[256 * h : 256 * h + width, :] = nn(pick, b_in[:, :width]).T.astype(BF16)
-    bbuf[r] = btw[pl.ds(pl.multiple_of(CSH * (c % 2), 64), CSH), :]
+        remote(b2.at[src], b2.at[src], bsend.at[i], brecv.at[src], r, src).wait()
+
+    pieces = nn(pick, b2[...].reshape(512, 128)).astype(BF16)
+    for j in range(4):
+        bbuf[r, :, 128 * j : 128 * j + 128] = pieces[128 * j : 128 * j + 128]
 
     bsends = []
 
@@ -352,11 +353,11 @@
         spread(r_z, r_x(r, d))
     spread(r_z, r_core)
 
-    def product(k, pair):
-        idx = zls[k] * 4 + pair
-        out[...] += nn(bbuf[idx], abuf[idx])
-
-    pair0 = y // 2
+    def product(k, y_half):
+        quad = zls[k] * 2 + y_half
+        b = btr[quad, pl.ds(pl.multiple_of(64 * (c % 2), 64), CSH), :]
+        out[...] += nn(b, abuf[pl.ds(4 * quad, 4)].reshape(256, RSH))
+
     for s in range(1, 5):
         for k in range(4):
             right, left = (4, 3) if k % 2 == 0 else (3, 4)
@@ -368,42 +369,47 @@
                 arrived(zls[k], y_of[s % 8])
                 if s < left:
                     pass_on(k, s, -1)
-            if s == 2:
-                product(k, pair0)
             if s == 3:
-                product(k, (pair0 + 1) % 4)
-                product(k, (pair0 + 3) % 4)
+                product(k, y // 4)
             if s == 4:
-                product(k, (pair0 + 2) % 4)
+                product(k, 1 - y // 4)
         if s == 1:
             for base in (r, r_z):
                 for d in (1, 3, 2):
                     b_arrived(r_x(base, d))
                     spread(r_x(base, d), r_core)
+        if s == 2:
             for base in (r, r_z):
                 for d in range(4):
                     row = r_x(base, d)
                     b_arrived(row + 1 - 2 * (row % 2))
-            prior_copy.wait()
+            m, p = iota((256, 256), 0), iota((256, 256), 1)
+            same = (p // 16 == (m // 4) % 16) & (p % 4 == m % 4) & ((p // 4) % 4 == m // 64)
+            pick = jnp.where(same, 1.0, 0.0).astype(BF16)
+
+            @pl.loop(0, 8)
+            def _(n):
+                rows = bbuf[:, pl.ds(pl.multiple_of(16 * n, 16), 16), :].reshape(256, 512)
+                btr[n] = nn(pick, rows).T.astype(BF16)
 
     for copy in sends + bsends:
         copy.wait_send()
 
 
 def per_device(design, nuisance_vals, arc_index, filter_taps, ordering, normal_prior):
-    coef = COEF_W * COLS
-    cols = jnp.pad(ordering[:coef].reshape(COLS, COEF_W), ((0, 0), (0, 512 - COEF_W)), constant_values=-1)
-    slots = jnp.concatenate(
-        [cols.reshape(128, 128), ordering[coef:].reshape(2, 128), jnp.full((6, 128), -1, jnp.int32)], 0
-    )
     vmem = pl.BlockSpec(memory_space=pltpu.VMEM)
     dma = pltpu.SemaphoreType.DMA
     result = pl.pallas_call(
         kernel,
         out_shape=jax.ShapeDtypeStruct((CSH, RSH), F32),
-        in_specs=[vmem] * 5 + [pl.BlockSpec(memory_space=pl.ANY)],
+        in_specs=[vmem] + [pl.BlockSpec(memory_space=pltpu.HBM)] * 4,
         out_specs=vmem,
         scratch_shapes=[
+            pltpu.VMEM((NPA, SEG), F32),
+            pltpu.VMEM((1, SEG), jnp.int32),
+            pltpu.VMEM((1, SEG), F32),
+            pltpu.VMEM((112, 128), jnp.int32),
+            pltpu.VMEM((136, 128), jnp.int32),
             pltpu.VMEM((512, SEG), BF16),
             pltpu.VMEM((512, SEG), BF16),
             pltpu.VMEM((8, SEG), F32),
@@ -414,12 +420,13 @@
             pltpu.VMEM((GROUPS, 256, 128 * GTILES), BF16),
             pltpu.VMEM((256, 128 * GTILES), BF16),
             pltpu.VMEM((256, 256), F32),
-            pltpu.VMEM((16, 16, 256), BF16),
-            pltpu.VMEM((16, 16, 256), BF16),
-            pltpu.VMEM((32, 16, 256), BF16),
-            pltpu.VMEM((RSH, SEG), BF16),
-            pltpu.VMEM((16, SEG, RSH), BF16),
-            pltpu.VMEM((16, CSH, SEG), BF16),
+            pltpu.VMEM((COLS, 16, 128), BF16),
+            pltpu.VMEM((ROWS, 2, 16, 128), BF16),
+            pltpu.VMEM((COLS, 16, 128), BF16),
+            pltpu.VMEM((COLS, 64, RSH), BF16),
+            pltpu.VMEM((ROWS, SEG, 512), BF16),
+            pltpu.VMEM((8, 512, 256), BF16),
+            dma((4,)),
             dma((2,)),
             dma((2,)),
             dma((COLS,)),
@@ -432,7 +439,6 @@
             dma((COLS,)),
             dma((20,)),
             dma((ROWS,)),
-            dma,
         ],
         compiler_params=pltpu.CompilerParams(
             collective_id=0, has_side_effects=True, vmem_limit_bytes=48 * 1024 * 1024
@@ -442,10 +448,9 @@
         nuisance_vals,
         arc_index.reshape(1, SEG),
         filter_taps.reshape(1, SEG),
-        slots,
-        normal_prior.T,
+        ordering.reshape(112, 128),
     )
-    return result.T
+    return normal_prior + result.T
 
 
 def solution(mesh):

time: 112 us -> 96.3 us (0.86)
  Pallas kernels: 103 us -> 91 us
  local copies, waits for them, and re-layouts: 7.15 us -> 3.71 us
  other arithmetic: 0.08 us -> 1.32 us
    pallas_call x1, Pallas kernels: 103 us -> 91 us  [per_device(): pl.pallas_call(kernel, out_shape=jax.ShapeDtypeStruct((CSH, RSH), F32), i...]
    unnamed x11 -> x12, local copies, waits for them, and re-layouts: 5.46 us -> 3.71 us
    add x0 -> x1, other arithmetic: none -> 1.32 us  [per_device(): return normal_prior + result.T]
where the time goes in v2:
time: 96.3 us; the launch traced here: 96.1 us
  Pallas kernels  91 us (94%)
  local copies, waits for them, and re-layouts  3.71 us (4%)
  other arithmetic  1.32 us (1%)
    pallas_call x1, Pallas kernels, per_device(): pl.pallas_call(kernel, out_shape=jax.ShapeDtypeStruct((CSH, RSH), F32), i...  91 us
    unnamed x12, local copies, waits for them, and re-layouts  3.71 us

profile of v2, /device:TPU:6, one launch (start us, length us, event | category | flops | bytes accessed | tf_op | source)
XLA Modules:
  0.0 96.1 jit_solution(10637820760134495593)
XLA Ops:
  0.0 0.0 copy-start
  0.0 0.9 copy-done
  0.9 0.0 copy-start.1
  0.9 0.8 copy-done.1
  1.7 0.0 copy-start.2
  1.7 0.7 copy-done.2
  2.4 0.0 copy-start.3
  2.4 0.7 copy-done.3
  3.1 0.0 copy-start.4
  3.1 0.7 copy-done.4
  3.7 0.0 copy-start.5
  3.7 91.0 %shard_map.64 = f32[448,896]{1,0:T(8,128)S(1)} custom-call(bf16[440,128]{1,0:T(8,128)(2,1)S(1)} %bitcast.6, f32[4,128]{1,0:T(4,128)S(1)} %copy-done.2, s32[1,128]{1,0:T(1,128)S(1)} %bitcast.8, f32[1,128]{1,0:T(1,128)S(1)} %bitcast.9, s32[112,128]{1,0:T(8,128)S(1)} %bitcast.7), custom_call_target="tpu_custom_call" | custom-call | tf_op jit(solution)/shard_map/pallas_call | solution.py:402
  94.8 0.0 copy-done.5
  94.8 1.3 %bitcast_add_fusion = f32[896,448]{0,1:T(8,128)} fusion(f32[896,448]{0,1:T(8,128)S(1)} %copy-done.5, f32[448,896]{1,0:T(8,128)S(1)} %shard_map.64), kind=kLoop, calls=%fused_computation | loop fusion | flops 401408 | bytes 4816896 | tf_op jit(solution)/shard_map/add | solution.py:453
Async XLA Ops:
  0.0 0.9 copy-start
  0.9 0.8 copy-start.1
  1.7 0.7 copy-start.2
  2.4 0.7 copy-start.3
  3.1 0.7 copy-start.4
  3.7 91.1 %copy-start.5 = (f32[896,448]{0,1:T(8,128)S(1)}, f32[896,448]{0,1:T(8,128)}, u32[]{:S(2)}) copy-start(f32[896,448]{0,1:T(8,128)} %param.11) | copy-start | bytes 4816900

commit v3 on v2

--- a/solution.py
+++ b/solution.py
@@ -46,6 +46,7 @@
     arcs_hbm,
     taps_hbm,
     ordering_hbm,
+    prior_hbm,
     out,
     vals,
     arcs,
@@ -65,10 +66,12 @@
     obuf,
     a2,
     b2,
-    abuf,
+    pbuf,
+    qbuf,
     bbuf,
     btr,
     load_sem,
+    prior_sem,
     hsend,
     hrecv,
     psend,
@@ -79,6 +82,10 @@
     brecv,
     gsend,
     grecv,
+    ssend,
+    srecv,
+    lsend,
+    lrecv,
     qsend,
     qrecv,
 ):
@@ -101,6 +108,8 @@
     ]
     for load in loads:
         load.start()
+    prior_load = pltpu.make_async_copy(prior_hbm, out, prior_sem)
+    prior_load.start()
 
     barrier = pltpu.get_barrier_semaphore()
 
@@ -115,7 +124,6 @@
     def _(i):
         tell(r, (c + i) % COLS)
 
-    out[...] = jnp.zeros((CSH, RSH), F32)
     own[...] = jnp.zeros((512, SEG), BF16)
     own[0:COEF_W, :] = design[...]
     for load in loads:
@@ -277,11 +285,12 @@
         remote(a2.at[src], a2.at[src], asend.at[i], arecv.at[src], src, c).wait()
 
     pieces = nn(pick, a2[...].reshape(512, 128)).astype(BF16)
-    for j in range(7):
-        abuf[c, :, 128 * j : 128 * j + 128] = pieces[64 * j : 64 * j + 64]
+    for j in range(6):
+        pbuf[c, :, 128 * j : 128 * j + 128] = pieces[64 * j : 64 * j + 64]
+    qbuf[c] = pieces[384:448]
 
     def chunk(zl, yy):
-        return abuf.at[zl * 8 + yy]
+        return pbuf.at[zl * 8 + yy]
 
     y_of = [(y + d) % 8 for d in range(8)]
     zls = [(zl0 + k) % 4 for k in range(4)]
@@ -304,6 +313,60 @@
     def arrived(zl, yy):
         remote(chunk(zl, yy), chunk(zl, yy), gsend.at[0], grecv.at[zl * 8 + yy], r, c).wait_recv()
 
+    qsends = []
+
+    def q_pass(dist, direction):
+        piece = qbuf.at[zl0 * 8 + y_of[(-direction * dist) % 8]]
+        copy = remote(
+            piece,
+            piece,
+            ssend.at[len(qsends)],
+            srecv.at[y_of[(-direction * dist) % 8]],
+            r,
+            zl0 * 8 + y_of[direction % 8],
+        )
+        copy.start()
+        qsends.append(copy)
+
+    def q_arrived(yy):
+        piece = qbuf.at[zl0 * 8 + yy]
+        remote(piece, piece, ssend.at[0], srecv.at[yy], r, c).wait_recv()
+
+    def q_step(s):
+        q_arrived(y_of[-s % 8])
+        if s < 4:
+            q_pass(s, 1)
+            q_arrived(y_of[s])
+            if s < 3:
+                q_pass(s, -1)
+
+    def level_copy(dist, up):
+        level = zl0 - dist if up else zl0 + dist
+        levels = qbuf.at[pl.ds(8 * level, 8)]
+        to = c + 8 if up else c - 8
+        return remote(levels, levels, lsend.at[2 * dist + int(up)], lrecv.at[level], r, to)
+
+    def level_goes(dist, up):
+        return (zl0 >= dist) & (zl0 < 3) if up else (zl0 <= 3 - dist) & (zl0 > 0)
+
+    def level_step(dist):
+        for up in (True, False):
+            if dist:
+                level = zl0 - dist if up else zl0 + dist
+
+                @pl.when(zl0 >= dist if up else zl0 <= 3 - dist)
+                def _():
+                    levels = qbuf.at[pl.ds(8 * level, 8)]
+                    remote(levels, levels, lsend.at[0], lrecv.at[level], r, c).wait_recv()
+
+            if dist < 3:
+
+                @pl.when(level_goes(dist, up))
+                def _():
+                    level_copy(dist, up).start()
+
+    q_pass(0, 1)
+    q_pass(0, -1)
     pass_on(0, 0, 1)
     pass_on(0, 0, -1)
     for k in (1, 3, 2):
@@ -343,20 +406,19 @@
         spread(r, r_x(r, d))
     spread(r, r_core)
 
-    for k in (1, 3, 2):
+    for n, k in enumerate((1, 3, 2)):
+        q_step(n + 1)
         arrived(zls[k], y)
         pass_on(k, 0, 1)
         pass_on(k, 0, -1)
-
-    b_arrived(r_z)
-    for d in (1, 3, 2):
-        spread(r_z, r_x(r, d))
-    spread(r_z, r_core)
+    q_step(4)
+    level_step(0)
 
     def product(k, y_half):
         quad = zls[k] * 2 + y_half
         b = btr[quad, pl.ds(pl.multiple_of(64 * (c % 2), 64), CSH), :]
-        out[...] += nn(b, abuf[pl.ds(4 * quad, 4)].reshape(256, RSH))
+        out[:, :768] += nn(b, pbuf[pl.ds(4 * quad, 4)].reshape(256, 768))
+        out[:, 768:] += nn(b, qbuf[pl.ds(4 * quad, 4)].reshape(256, 128))
 
     for s in range(1, 5):
         for k in range(4):
@@ -369,16 +431,23 @@
                 arrived(zls[k], y_of[s % 8])
                 if s < left:
                     pass_on(k, s, -1)
-            if s == 3:
-                product(k, y // 4)
             if s == 4:
                 product(k, 1 - y // 4)
+        if s < 4:
+            level_step(s)
         if s == 1:
-            for base in (r, r_z):
-                for d in (1, 3, 2):
-                    b_arrived(r_x(base, d))
-                    spread(r_x(base, d), r_core)
+            for d in (1, 3, 2):
+                b_arrived(r_x(r, d))
+                spread(r_x(r, d), r_core)
+            b_arrived(r_z)
+            for d in (1, 3, 2):
+                spread(r_z, r_x(r, d))
+            spread(r_z, r_core)
         if s == 2:
+            for d in (1, 3, 2):
+                b_arrived(r_x(r_z, d))
+                spread(r_x(r_z, d), r_core)
+        if s == 3:
             for base in (r, r_z):
                 for d in range(4):
                     row = r_x(base, d)
@@ -392,8 +461,18 @@
                 rows = bbuf[:, pl.ds(pl.multiple_of(16 * n, 16), 16), :].reshape(256, 512)
                 btr[n] = nn(pick, rows).T.astype(BF16)
 
-    for copy in sends + bsends:
+            prior_load.wait()
+            for k in range(4):
+                product(k, y // 4)
+
+    for copy in sends + bsends + qsends:
         copy.wait_send()
+    for dist in range(3):
+        for up in (True, False):
+
+            @pl.when(level_goes(dist, up))
+            def _():
+                level_copy(dist, up).wait_send()
 
 
 def per_device(design, nuisance_vals, arc_index, filter_taps, ordering, normal_prior):
@@ -402,7 +481,7 @@
     result = pl.pallas_call(
         kernel,
         out_shape=jax.ShapeDtypeStruct((CSH, RSH), F32),
-        in_specs=[vmem] + [pl.BlockSpec(memory_space=pltpu.HBM)] * 4,
+        in_specs=[vmem] + [pl.BlockSpec(memory_space=pl.ANY)] * 5,
         out_specs=vmem,
         scratch_shapes=[
             pltpu.VMEM((NPA, SEG), F32),
@@ -423,10 +502,12 @@
             pltpu.VMEM((COLS, 16, 128), BF16),
             pltpu.VMEM((ROWS, 2, 16, 128), BF16),
             pltpu.VMEM((COLS, 16, 128), BF16),
-            pltpu.VMEM((COLS, 64, RSH), BF16),
+            pltpu.VMEM((COLS, 64, 768), BF16),
+            pltpu.VMEM((COLS, 64, 128), BF16),
             pltpu.VMEM((ROWS, SEG, 512), BF16),
             pltpu.VMEM((8, 512, 256), BF16),
             dma((4,)),
+            dma,
             dma((2,)),
             dma((2,)),
             dma((COLS,)),
@@ -437,11 +518,15 @@
             dma((COLS,)),
             dma((40,)),
             dma((COLS,)),
+            dma((8,)),
+            dma((8,)),
+            dma((6,)),
+            dma((4,)),
             dma((20,)),
             dma((ROWS,)),
         ],
         compiler_params=pltpu.CompilerParams(
-            collective_id=0, has_side_effects=True, vmem_limit_bytes=48 * 1024 * 1024
+            collective_id=0, has_side_effects=True, vmem_limit_bytes=60 * 1024 * 1024
         ),
     )(
         design.T,
@@ -449,8 +534,9 @@
         arc_index.reshape(1, SEG),
         filter_taps.reshape(1, SEG),
         ordering.reshape(112, 128),
+        normal_prior.T,
     )
-    return normal_prior + result.T
+    return result.T
 
 
 def solution(mesh):

time: 96.3 us -> 91.9 us (0.954)
  Pallas kernels: 91 us -> 89 us
  other arithmetic: 1.32 us -> 0 us
  local copies, waits for them, and re-layouts: 3.71 us -> 2.68 us
    pallas_call x1, Pallas kernels: 91 us -> 89 us  [per_device(): pl.pallas_call(kernel, out_shape=jax.ShapeDtypeStruct((CSH, RSH), F32), i...]
    add x1 -> x0, other arithmetic: 1.32 us -> none  [per_device(): return normal_prior + result.T]
    unnamed x12 -> x1, local copies, waits for them, and re-layouts: 3.71 us -> 2.68 us
where the time goes in v3:
time: 91.9 us; the launch traced here: 91.7 us
  Pallas kernels  89 us (97%)
  local copies, waits for them, and re-layouts  2.68 us (3%)
    pallas_call x1, Pallas kernels, per_device(): pl.pallas_call(kernel, out_shape=jax.ShapeDtypeStruct((CSH, RSH), F32), i...  89 us
    unnamed x1, local copies, waits for them, and re-layouts  2.68 us

profile of v3, /device:TPU:6, one launch (start us, length us, event | category | flops | bytes accessed | tf_op | source)
XLA Modules:
  0.0 91.7 jit_solution(12124601647237837483)
XLA Ops:
  0.0 89.0 %shard_map.64 = f32[448,896]{1,0:T(8,128)} custom-call(bf16[440,128]{1,0:T(8,128)(2,1)} %bitcast.8, f32[4,128]{1,0:T(4,128)} %vals_hbm.1, s32[1,128]{1,0:T(1,128)} %bitcast.10, f32[1,128]{1,0:T(1,128)} %bitcast.11, s32[112,128]{1,0:T(8,128)} %bitcast.9, f32[448,896]{1,0:T(8,128)} %bitcast.7), custom_call_target="tpu_custom_call" | custom-call | tf_op jit(solution)/shard_map/pallas_call | solution.py:481
  89.0 2.7 %copy.8 = f32[896,448]{0,1:T(8,128)} copy(f32[896,448]{0,1:T(8,128)} %bitcast.6) | data formatting | bytes 3211264

commit v4 on v3

--- a/solution.py
+++ b/solution.py
@@ -42,16 +42,9 @@
 
 def kernel(
     design,
-    vals_hbm,
-    arcs_hbm,
-    taps_hbm,
-    ordering_hbm,
+    small,
     prior_hbm,
     out,
-    vals,
-    arcs,
-    taps,
-    ordering,
     slots,
     own,
     halo,
@@ -70,7 +63,6 @@
     qbuf,
     bbuf,
     btr,
-    load_sem,
     prior_sem,
     hsend,
     hrecv,
@@ -100,14 +92,7 @@
     def r_x(row, d):
         return row - 2 * xi + 2 * ((xi + d) % 4)
 
-    loads = [
-        pltpu.make_async_copy(src, dst, load_sem.at[n])
-        for n, (src, dst) in enumerate(
-            ((vals_hbm, vals), (arcs_hbm, arcs), (taps_hbm, taps), (ordering_hbm, ordering))
-        )
-    ]
-    for load in loads:
-        load.start()
+    ordering = small[0:112]
     prior_load = pltpu.make_async_copy(prior_hbm, out, prior_sem)
     prior_load.start()
 
@@ -126,10 +111,8 @@
 
     own[...] = jnp.zeros((512, SEG), BF16)
     own[0:COEF_W, :] = design[...]
-    for load in loads:
-        load.wait()
-    nown[0:4, :] = vals[...]
-    nown[4:8, :] = jnp.broadcast_to(arcs[...].astype(F32), (4, SEG))
+    nown[0:4, :] = small[112:116]
+    nown[4:8, :] = jnp.broadcast_to(small[116:117], (4, SEG))
 
     pl.semaphore_wait(barrier, ROWS + COLS - 2)
 
@@ -150,20 +133,19 @@
                 line = jnp.where(lane >= off, line, ordering[tile + 1 : tile + 2])
                 line = pltpu.roll(line, 128 - off, 1)
             if q == 3:
-                line = jnp.where(lane < COEF_W - 384, line, -1)
+                line = jnp.where(lane < COEF_W - 384, line, -1.0)
             slots[4 * src + q : 4 * src + q + 1] = line
     slots[128:130] = ordering[COLS * COEF_W // 128 :]
 
     hp = (iota((256, 128), 0) // 4).astype(F32)
     lp = iota((256, 128), 0).astype(F32)
 
-    def factors(rows):
-        s = rows.astype(F32)
+    def factors(s):
         cc = jnp.floor((s + 0.5) * (1.0 / CSH))
         odd = cc - 2.0 * jnp.floor(cc * 0.5)
         u = s - cc * CSH + 64.0 * odd
         h = jnp.floor((u + 0.5) * (1.0 / 256.0))
-        return jnp.where(rows < 0, -1.0, 2.0 * cc + h), u - 256.0 * h
+        return jnp.where(s < 0.0, -1.0, 2.0 * cc + h), u - 256.0 * h
 
     def one_hot(row, pattern):
         return jnp.where(jnp.broadcast_to(row, pattern.shape) == pattern, 1.0, 0.0).astype(BF16)
@@ -175,7 +157,7 @@
             hot_hi[g, :, 128 * i : 128 * i + 128] = one_hot(hi[i : i + 1], hp)
             hot_lo[g, :, 128 * i : 128 * i + 128] = one_hot(lo[i : i + 1], lp)
 
-    line = jnp.concatenate([taps[...], jnp.zeros((1, SEG), F32)], 1)
+    line = jnp.concatenate([small[117:118], jnp.zeros((1, SEG), F32)], 1)
     band = pltpu.roll(jnp.broadcast_to(line, (SEG, 2 * SEG)), 0, 1, stride=1, stride_axis=0)
     has_past = jnp.where(r > 0, 1.0, 0.0).astype(F32)
     band_now, band_past = band[:, :SEG], band[:, SEG:] * has_past
@@ -401,7 +383,6 @@
     def b_arrived(row):
         remote(bbuf.at[row], bbuf.at[row], qsend.at[0], qrecv.at[row], r, c).wait_recv()
 
-    spread(r, r_z)
     for d in (1, 3, 2):
         spread(r, r_x(r, d))
     spread(r, r_core)
@@ -412,6 +393,7 @@
         pass_on(k, 0, 1)
         pass_on(k, 0, -1)
     q_step(4)
+    spread(r, r_z)
     level_step(0)
 
     def product(k, y_half):
@@ -478,17 +460,23 @@
 def per_device(design, nuisance_vals, arc_index, filter_taps, ordering, normal_prior):
     vmem = pl.BlockSpec(memory_space=pltpu.VMEM)
     dma = pltpu.SemaphoreType.DMA
+    small = jnp.concatenate(
+        [
+            ordering.astype(F32).reshape(112, SEG),
+            nuisance_vals,
+            arc_index.astype(F32).reshape(1, SEG),
+            filter_taps.reshape(1, SEG),
+            jnp.zeros((2, SEG), F32),
+        ],
+        0,
+    )
     result = pl.pallas_call(
         kernel,
         out_shape=jax.ShapeDtypeStruct((CSH, RSH), F32),
-        in_specs=[vmem] + [pl.BlockSpec(memory_space=pl.ANY)] * 5,
+        in_specs=[vmem, vmem, pl.BlockSpec(memory_space=pl.ANY)],
         out_specs=vmem,
         scratch_shapes=[
-            pltpu.VMEM((NPA, SEG), F32),
-            pltpu.VMEM((1, SEG), jnp.int32),
-            pltpu.VMEM((1, SEG), F32),
-            pltpu.VMEM((112, 128), jnp.int32),
-            pltpu.VMEM((136, 128), jnp.int32),
+            pltpu.VMEM((136, 128), F32),
             pltpu.VMEM((512, SEG), BF16),
             pltpu.VMEM((512, SEG), BF16),
             pltpu.VMEM((8, SEG), F32),
@@ -506,7 +494,6 @@
             pltpu.VMEM((COLS, 64, 128), BF16),
             pltpu.VMEM((ROWS, SEG, 512), BF16),
             pltpu.VMEM((8, 512, 256), BF16),
-            dma((4,)),
             dma,
             dma((2,)),
             dma((2,)),
@@ -526,14 +513,11 @@
             dma((ROWS,)),
         ],
         compiler_params=pltpu.CompilerParams(
-            collective_id=0, has_side_effects=True, vmem_limit_bytes=60 * 1024 * 1024
+            collective_id=0, has_side_effects=True, vmem_limit_bytes=52 * 1024 * 1024
         ),
     )(
         design.T,
-        nuisance_vals,
-        arc_index.reshape(1, SEG),
-        filter_taps.reshape(1, SEG),
-        ordering.reshape(112, 128),
+        small,
         normal_prior.T,
     )
     return result.T

time: 91.9 us -> 86.9 us (0.946)
  Pallas kernels: 89 us -> 81.7 us
  other arithmetic: 0 us -> 1.48 us
    pallas_call x1, Pallas kernels: 89 us -> 81.7 us  [per_device(): pl.pallas_call(kernel, out_shape=jax.ShapeDtypeStruct((CSH, RSH), F32), i...]
    reshape x0 -> x2, other arithmetic: none -> 1.48 us  [the longest x1 0.82 us: per_device(): ordering.astype(F32).reshape(112, SEG)]
    unnamed x1 -> x3, local copies, waits for them, and re-layouts: 2.68 us -> 2.05 us
where the time goes in v4:
time: 86.9 us; the launch traced here: 85.9 us
  Pallas kernels  81.7 us (94%)
  local copies, waits for them, and re-layouts  2.76 us (3%)
  other arithmetic  1.48 us (2%)
    pallas_call x1, Pallas kernels, per_device(): pl.pallas_call(kernel, out_shape=jax.ShapeDtypeStruct((CSH, RSH), F32), i...  81.7 us
    unnamed x3, local copies, waits for them, and re-layouts  2.05 us

profile of v4, /device:TPU:6, one launch (start us, length us, event | category | flops | bytes accessed | tf_op | source)
XLA Modules:
  0.0 85.9 jit_solution(12483486134804673707)
XLA Ops:
  0.0 0.7 convert_bitcast_fusion.1
  0.7 0.8 convert_bitcast_fusion
  1.5 0.7 concatenate.3.small
  2.2 0.0 copy-start
  2.2 0.9 %copy-done = bf16[128,440]{0,1:T(8,128)(2,1)S(1)} copy-done((bf16[128,440]{0,1:T(8,128)(2,1)S(1)}, bf16[128,440]{0,1:T(8,128)(2,1)}, u32[]{:S(2)}) %copy-start) | copy-done | bytes 112664
  3.1 81.7 %shard_map.64 = f32[448,896]{1,0:T(8,128)S(1)} custom-call(bf16[440,128]{1,0:T(8,128)(2,1)S(1)} %bitcast.9, f32[120,128]{1,0:T(8,128)S(1)} %concatenate.3.small, f32[448,896]{1,0:T(8,128)} %bitcast.10), custom_call_target="tpu_custom_call" | custom-call | tf_op jit(solution)/shard_map/pallas_call | solution.py:473
  84.8 1.2 %copy.8 = f32[896,448]{0,1:T(8,128)} copy(f32[896,448]{0,1:T(8,128)S(1)} %bitcast.8) | data formatting | bytes 3211264
  (1 shorter events, 0.0 us)
Async XLA Ops:
  2.2 0.9 %copy-start = (bf16[128,440]{0,1:T(8,128)(2,1)S(1)}, bf16[128,440]{0,1:T(8,128)(2,1)}, u32[]{:S(2)}) copy-start(bf16[128,440]{0,1:T(8,128)(2,1)} %param.6) | copy-start | bytes 337924

commit v5 on v4

--- a/solution.py
+++ b/solution.py
@@ -393,8 +393,8 @@
         pass_on(k, 0, 1)
         pass_on(k, 0, -1)
     q_step(4)
+    level_step(0)
     spread(r, r_z)
-    level_step(0)
 
     def product(k, y_half):
         quad = zls[k] * 2 + y_half

time: 86.9 us -> 88.8 us (1.022)
  the two profiles are of different devices: /device:TPU:6 before, /device:TPU:20 now
where the time goes in v5:
time: 88.8 us; the launch traced here: 88.6 us
  Pallas kernels  84.4 us (95%)
  local copies, waits for them, and re-layouts  2.76 us (3%)
  other arithmetic  1.48 us (2%)
    pallas_call x1, Pallas kernels, per_device(): pl.pallas_call(kernel, out_shape=jax.ShapeDtypeStruct((CSH, RSH), F32), i...  84.4 us
    unnamed x3, local copies, waits for them, and re-layouts  2.05 us

profile of v5, /device:TPU:20, one launch (start us, length us, event | category | flops | bytes accessed | tf_op | source)
XLA Modules:
  0.0 88.6 jit_solution(8697599956097993120)
XLA Ops:
  0.0 0.7 convert_bitcast_fusion.1
  0.7 0.8 convert_bitcast_fusion
  1.5 0.7 concatenate.3.small
  2.2 0.0 copy-start
  2.2 0.9 %copy-done = bf16[128,440]{0,1:T(8,128)(2,1)S(1)} copy-done((bf16[128,440]{0,1:T(8,128)(2,1)S(1)}, bf16[128,440]{0,1:T(8,128)(2,1)}, u32[]{:S(2)}) %copy-start) | copy-done | bytes 112664
  3.1 84.4 %shard_map.64 = f32[448,896]{1,0:T(8,128)S(1)} custom-call(bf16[440,128]{1,0:T(8,128)(2,1)S(1)} %bitcast.9, f32[120,128]{1,0:T(8,128)S(1)} %concatenate.3.small, f32[448,896]{1,0:T(8,128)} %bitcast.10), custom_call_target="tpu_custom_call" | custom-call | tf_op jit(solution)/shard_map/pallas_call | solution.py:473
  87.4 1.2 %copy.8 = f32[896,448]{0,1:T(8,128)} copy(f32[896,448]{0,1:T(8,128)S(1)} %bitcast.8) | data formatting | bytes 3211264
  (1 shorter events, 0.0 us)
Async XLA Ops:
  2.2 0.9 %copy-start = (bf16[128,440]{0,1:T(8,128)(2,1)S(1)}, bf16[128,440]{0,1:T(8,128)(2,1)}, u32[]{:S(2)}) copy-start(bf16[128,440]{0,1:T(8,128)(2,1)} %param.6) | copy-start | bytes 337924

commit v6 on v5

--- a/solution.py
+++ b/solution.py
@@ -392,9 +392,9 @@
         arrived(zls[k], y)
         pass_on(k, 0, 1)
         pass_on(k, 0, -1)
+    spread(r, r_z)
     q_step(4)
     level_step(0)
-    spread(r, r_z)
 
     def product(k, y_half):
         quad = zls[k] * 2 + y_half

time: 88.8 us -> 86.3 us (0.972)
  the two profiles are of different devices: /device:TPU:20 before, /device:TPU:6 now
where the time goes in v6:
time: 86.3 us; the launch traced here: 85.9 us
  Pallas kernels  81.7 us (95%)
  local copies, waits for them, and re-layouts  2.76 us (3%)
  other arithmetic  1.48 us (2%)
    pallas_call x1, Pallas kernels, per_device(): pl.pallas_call(kernel, out_shape=jax.ShapeDtypeStruct((CSH, RSH), F32), i...  81.7 us
    unnamed x3, local copies, waits for them, and re-layouts  2.05 us

profile of v6, /device:TPU:6, one launch (start us, length us, event | category | flops | bytes accessed | tf_op | source)
XLA Modules:
  0.0 85.9 jit_solution(15286540962226241014)
XLA Ops:
  0.0 0.7 convert_bitcast_fusion.1
  0.7 0.8 convert_bitcast_fusion
  1.5 0.7 concatenate.3.small
  2.2 0.0 copy-start
  2.2 0.9 %copy-done = bf16[128,440]{0,1:T(8,128)(2,1)S(1)} copy-done((bf16[128,440]{0,1:T(8,128)(2,1)S(1)}, bf16[128,440]{0,1:T(8,128)(2,1)}, u32[]{:S(2)}) %copy-start) | copy-done | bytes 112664
  3.1 81.7 %shard_map.64 = f32[448,896]{1,0:T(8,128)S(1)} custom-call(bf16[440,128]{1,0:T(8,128)(2,1)S(1)} %bitcast.9, f32[120,128]{1,0:T(8,128)S(1)} %concatenate.3.small, f32[448,896]{1,0:T(8,128)} %bitcast.10), custom_call_target="tpu_custom_call" | custom-call | tf_op jit(solution)/shard_map/pallas_call | solution.py:473
  84.8 1.2 %copy.8 = f32[896,448]{0,1:T(8,128)} copy(f32[896,448]{0,1:T(8,128)S(1)} %bitcast.8) | data formatting | bytes 3211264
  (1 shorter events, 0.0 us)
Async XLA Ops:
  2.2 0.9 %copy-start = (bf16[128,440]{0,1:T(8,128)(2,1)S(1)}, bf16[128,440]{0,1:T(8,128)(2,1)}, u32[]{:S(2)}) copy-start(bf16[128,440]{0,1:T(8,128)(2,1)} %param.6) | copy-start | bytes 337924
